TPU v7x, 256 devices: a whole 4x4x8 slice. The times are simulated.
256 devices in a mesh: blk: 16 (over z, x_hi), dp: 16 (over x_lo, y, core).
Axes of the slice: x: 4 (x_hi: 2, x_lo: 2; x = x_hi * 2 + x_lo), y: 4, z: 8, core: 2. Of those that a mesh axis runs over, the one named last changes fastest.
Arguments:
- score_feats: bfloat16 [16, 3840, 1024], P('dp', 'blk'), may hold values from -6 to 6
- audio_feats: bfloat16 [16, 3840, 1024], P('dp', 'blk'), may hold values from -6 to 6
- score_weight: bfloat16 [1024, 1024], replicated, may hold values from -0.1875 to 0.1875
- audio_weight: bfloat16 [1024, 1024], replicated, may hold values from -0.1875 to 0.1875
- log_temp: float32 [1], replicated, may hold values from 1.6 to 3
- logit_bias: float32 [1], replicated, may hold values from -3 to -1
- loss_scale: float32 [1], replicated, may hold values from 150000 to 400000
Outputs:
- score_feat_grad: bfloat16 [16, 3840, 1024], P('dp', 'blk')
- audio_feat_grad: bfloat16 [16, 3840, 1024], P('dp', 'blk')
- score_weight_grad: float32 [1024, 1024], P('blk')
- audio_weight_grad: float32 [1024, 1024], P('blk')
All inputs are finite; a program needn't handle non-finite values.
Results may differ from a plain program's by a relative error of at most 0.023.
Values may be sent and summed in bfloat16 or wider, within the bound.
A program may use at most 128 MiB of HBM per device.

v0:
```python
import jax
import jax.numpy as jnp
from jax import lax
from jax.sharding import PartitionSpec as P


def tower_forward(features, weights):
    projected = jnp.dot(features, weights, preferred_element_type=jnp.float32)
    norm_vals = jnp.sqrt(jnp.sum(projected * projected, axis=-1, keepdims=True) + 1e-06)
    return (projected / norm_vals, norm_vals)


def unit_grad(unit_vec, norm_vals, grad_emb):
    radial = jnp.sum(unit_vec * grad_emb, axis=-1, keepdims=True)
    return ((grad_emb - unit_vec * radial) / norm_vals).astype(jnp.bfloat16)


def logit_tile(left_emb, right_emb, left_first, temper, bias_value):
    similarity = jnp.dot(left_emb, right_emb.T, preferred_element_type=jnp.float32)
    logits = temper * similarity + bias_value
    row_ids = lax.broadcasted_iota(jnp.int32, logits.shape, 0) + left_first
    col_ids = lax.broadcasted_iota(jnp.int32, logits.shape, 1)
    targets = (row_ids == col_ids).astype(jnp.float32)
    return (jax.nn.sigmoid(logits) - targets).astype(jnp.bfloat16)


def body(score_feats, audio_feats, score_weight, audio_weight, log_temp, logit_bias, loss_scale):
    score_feat = score_feats[0]
    audio_feat = audio_feats[0]
    row_count = score_feat.shape[0]
    emb_width = score_weight.shape[1]
    cycle_size = lax.axis_size("blk")
    groups = lax.axis_size("dp")
    own_first = lax.axis_index("blk") * row_count
    temper = jnp.exp(log_temp[0])
    bias_value = logit_bias[0]
    factor = loss_scale[0] * temper / (groups * row_count * cycle_size)
    score_unit, score_len = tower_forward(score_feat, score_weight)
    audio_unit, audio_len = tower_forward(audio_feat, audio_weight)
    score_emb = score_unit.astype(jnp.bfloat16)
    audio_emb = audio_unit.astype(jnp.bfloat16)
    gathered = lax.all_gather(audio_emb, "blk", axis=0, tiled=True)
    logit_grad = logit_tile(score_emb, gathered, own_first, temper, bias_value)
    score_emb_grad = factor * jnp.dot(logit_grad, gathered, preferred_element_type=jnp.float32)
    audio_emb_grad = factor * lax.psum_scatter(
        jnp.dot(logit_grad.T, score_emb, preferred_element_type=jnp.float32).astype(jnp.bfloat16),
        "blk",
        scatter_dimension=0,
        tiled=True,
    ).astype(jnp.float32)
    score_proj_grad = unit_grad(score_unit, score_len, score_emb_grad)
    audio_proj_grad = unit_grad(audio_unit, audio_len, audio_emb_grad)
    score_back = jnp.dot(
        score_proj_grad, score_weight.T, preferred_element_type=jnp.float32
    ).astype(jnp.bfloat16)
    audio_back = jnp.dot(
        audio_proj_grad, audio_weight.T, preferred_element_type=jnp.float32
    ).astype(jnp.bfloat16)
    score_rows = jnp.dot(score_feat.T, score_proj_grad, preferred_element_type=jnp.float32)
    audio_rows = jnp.dot(audio_feat.T, audio_proj_grad, preferred_element_type=jnp.float32)
    reduced = lax.psum_scatter(
        jnp.concatenate([score_rows, audio_rows], axis=1).astype(jnp.bfloat16),
        "blk",
        scatter_dimension=0,
        tiled=True,
    )
    summed = lax.psum(reduced, "dp").astype(jnp.float32)
    return (score_back[None], audio_back[None], summed[:, :emb_width], summed[:, emb_width:])


def solution(mesh):
    in_specs = (P("dp", "blk", None), P("dp", "blk", None), P(), P(), P(), P(), P())
    out_specs = (P("dp", "blk", None), P("dp", "blk", None), P("blk", None), P("blk", None))
    return jax.shard_map(body, mesh=mesh, in_specs=in_specs, out_specs=out_specs, check_vma=False)
```

profile of v0, /device:TPU:1, one launch (start us, length us, event | category | flops | bytes accessed | tf_op | source)
XLA Modules:
  0.0 739.5 jit_solution(5328706479058241722)
XLA Ops:
  7.2 0.0 all-gather.2.cloned.1.call-start
  7.2 2.6 multiply_reduce_fusion.2
  9.9 0.9 fusion.17
  10.8 0.0 all-gather.2.cloned.1.call-update
  10.8 0.0 reduce-scatter.5.cloned.1.call-start
  12.3 2.7 multiply_reduce_fusion.3
  15.0 130.3 %all-gather.2.cloned.1.call-done = bf16[3840,1024]{1,0:T(8,128)(2,1)} async-done(((bf16[240,1024]{1,0:T(8,128)(2,1)}), bf16[3840,1024]{1,0:T(8,128)(2,1)}) %all-gather.2.cloned.1.call-update) | async-done | bytes 7864336 | tf_op jit(solution)/shard_map/all_gather | solution.py:42
  145.4 6.9 fusion.6
  152.3 1.2 copy-done.4
  153.5 5.4 convolution_convert_fusion
  158.9 0.0 reduce-scatter.5.cloned.1.call-update
  158.9 0.0 reduce-scatter.7.cloned.1.call-start
  159.7 6.2 multiply_reduce_fusion.1
  165.9 0.2 divide_convert_fusion.1
  166.2 0.8 copy-done.6
  166.9 2.1 convert_bitcast_fusion.1
  169.1 208.9 %reduce-scatter.5.cloned.1.call-done = bf16[240,1024]{1,0:T(8,128)(2,1)} async-done(((bf16[3840,1024]{1,0:T(8,128)(2,1)}), bf16[240,1024]{1,0:T(8,128)(2,1)}) %reduce-scatter.5.cloned.1.call-update) | async-done | bytes 491536 | tf_op jit(solution)/shard_map/reduce_scatter | solution.py:45
  377.9 1.3 multiply_reduce_fusion
  379.2 2.2 convert_bitcast_fusion
  381.5 2.5 pad_maximum_fusion
  383.9 6.5 copy.15
  390.5 0.0 reduce-scatter.7.cloned.1.call-update
  390.5 0.0 all-reduce.2.cloned.1.call-start
  390.5 2.5 fusion.7
  393.1 207.2 %reduce-scatter.7.cloned.1.call-done = bf16[64,2048]{1,0:T(8,128)(2,1)} async-done(((bf16[1024,2048]{1,0:T(8,128)(2,1)}), bf16[64,2048]{1,0:T(8,128)(2,1)}) %reduce-scatter.7.cloned.1.call-update) | async-done | bytes 262160
  600.3 2.0 copy.16
  602.3 0.0 all-reduce.2.cloned.1.call-update
  602.3 3.3 fusion.8
  605.6 122.6 %all-reduce.2.cloned.1.call-done = bf16[64,2048]{0,1:T(8,128)(2,1)} async-done(((bf16[64,2048]{0,1:T(8,128)(2,1)}), bf16[64,2048]{0,1:T(8,128)(2,1)}) %all-reduce.2.cloned.1.call-update) | async-done | bytes 262160 | tf_op jit(solution)/shard_map/psum | solution.py:67
  728.2 1.9 fusion.18
  730.1 1.9 copy.13
  732.1 0.9 copy.14
  (15 shorter events, 0.1 us)
Async XLA Ops:
  7.2 5.1 copy-start
  7.2 138.2 %all-gather.2.cloned.1.call-start = ((), (), s32[]{:S(2)}) async-start(), calls=%async_computation.2 | async-start | bytes 8355840 | tf_op jit(solution)/shard_map/all_gather | solution.py:42
  10.8 367.1 %reduce-scatter.5.cloned.1.call-start = ((), (), s32[]{:S(2)}) async-start(), calls=%async_computation.3 | async-start | bytes 8355840 | tf_op jit(solution)/shard_map/reduce_scatter | solution.py:45
  145.4 8.1 %copy-start.1 = (f32[240,1024]{1,0:T(8,128)S(1)}, f32[240,1024]{1,0:T(8,128)}, u32[]{:S(2)}) copy-start(f32[240,1024]{1,0:T(8,128)} %get-tuple-element.17) | copy-start | bytes 2949124
  152.2 1.3 copy-start.4
  158.9 441.4 %reduce-scatter.7.cloned.1.call-start = ((), (), s32[]{:S(2)}) async-start(), calls=%async_computation.5 | async-start | bytes 4456448
  159.6 6.3 copy-start.2
  159.6 7.3 copy-start.5
  166.1 0.8 copy-start.6
  379.2 2.2 copy-start.3
  390.5 337.7 %all-reduce.2.cloned.1.call-start = ((), (), s32[]{:S(2)}) async-start(), calls=%async_computation.4 | async-start | bytes 1048576 | tf_op jit(solution)/shard_map/psum | solution.py:67
Sparse Core Ops, SparseCore 0:
  11.2 134.1 all-gather.1
  159.1 218.8 reduce-scatter.4
  390.6 209.6 reduce-scatter.6
  603.0 125.1 all-reduce.1
where the time goes:
time: 740 us; the launch traced here: 739 us
  waiting for transfers between devices  669 us (90%)
  matrix products  34.1 us (5%)
  between operations  15.9 us (2%)
  local copies, waits for them, and re-layouts  15.3 us (2%)
    reduce_scatter x1, waiting for transfers between devices, body(): lax.psum_scatter(jnp.dot(logit_grad.T, score_emb, preferred_element_type=...  209 us
    unnamed x5, waiting for transfers between devices  207 us
    all_gather x1, waiting for transfers between devices, body(): gathered = lax.all_gather(audio_emb, 'blk', axis=0, tiled=True)  130 us
    psum x1, waiting for transfers between devices, body(): summed = lax.psum(reduced, 'dp').astype(jnp.float32)  123 us
  transfers between devices with their start and end apart: 4, of which 4 were waited for; matrix products, arithmetic and copies ran while one was open for 2% of the time, Pallas kernels for 0%

commit v1 on v0

v1 whole, which is shorter than its diff:
```python
import functools

import jax
import jax.numpy as jnp
from jax import lax
from jax.experimental import pallas as pl
from jax.experimental.pallas import tpu as pltpu
from jax.sharding import PartitionSpec as P

MESH = pl.DeviceIdType.MESH
BF = jnp.bfloat16
F32 = jnp.float32
ROWS = 240
WIDTH = 1024
TILE = 256
STEP = 48

LOW = ((0, 64), (64, 48))
HIGH = ((112, 64), (176, 64))
CHUNKS = LOW + HIGH
PLUS, MINUS = 0, 1
GATHER_FAR = {PLUS: HIGH, MINUS: LOW}
SUM_FAR = {PLUS: LOW, MINUS: HIGH}


def dot_nn(a, b):
    return lax.dot_general(a, b, (((1,), (0,)), ((), ())), preferred_element_type=F32)


def dot_nt(a, b):
    return lax.dot_general(a, b, (((1,), (1,)), ((), ())), preferred_element_type=F32)


def dot_tn(a, b):
    return lax.dot_general(a, b, (((0,), (0,)), ((), ())), preferred_element_type=F32)


def tile_at(index, size):
    return pl.ds(pl.multiple_of(index * size, size), size)


def kernel(
    groups_rows,
    feat_s, feat_a, weight_s, weight_a, temp_ref, bias_ref, scale_ref,
    back_s, back_a, rows_s, rows_a,
    unit, length, audio, score, grad_t, part, ring, side_out, side_in, emb_grad, proj_grad,
    outer, core_in, half, y_in, x_in, y_sum, x_sum, x_in2, y_in2, z_out, z_in, done,
    gather_send, gather_recv, ring_send, ring_recv, side_send, side_recv,
    core_send, core_recv, one_send, one_recv, two_send, two_recv, z_send, z_recv, all_send, all_recv,
):
    blk, dp = lax.axis_index("blk"), lax.axis_index("dp")
    zz, xh = blk // 2, lax.rem(blk, 2)
    xl, yy, core = dp // 8, lax.rem(dp // 2, 4), lax.rem(dp, 2)
    xx = xh * 2 + xl

    def device(dx=0, dy=0, dz=0, dc=0):
        x = lax.rem(xx + dx, 4)
        y = lax.rem(yy + dy, 4)
        z = lax.rem(zz + dz, 8)
        c = lax.rem(core + dc, 2)
        return {"blk": z * 2 + x // 2, "dp": (lax.rem(x, 2) * 4 + y) * 2 + c}

    def flat_dp(offset):
        return {"blk": blk, "dp": lax.rem(dp + offset, 16)}

    def remote(src, dst, send, recv, target):
        return pltpu.make_async_remote_copy(
            src_ref=src, dst_ref=dst, send_sem=send, recv_sem=recv, device_id=target, device_id_type=MESH
        )

    barrier = pltpu.get_barrier_semaphore()
    peers = [device(dz=k) for k in range(1, 8)] + [flat_dp(k) for k in range(1, 16)]
    peers += [device(dx=k) for k in (1, 2, 3)]
    for peer in peers:
        pl.semaphore_signal(barrier, inc=1, device_id=peer, device_id_type=MESH)

    temper = jnp.exp(jnp.full((1, 1), temp_ref[0], F32))
    bias = bias_ref[0]
    factor = scale_ref[0] * temper / groups_rows

    pending = []

    def launch(copy):
        copy.start()
        pending.append(copy)

    def rows_in(first, count, fn):
        def step(i, carry):
            fn(pl.ds(pl.multiple_of(first + i * 16, 16), 16))
            return carry

        lax.fori_loop(0, count // 16, step, 0, unroll=True)

    def project(tower, feat, weight, store):
        def column(j, carry):
            cols = tile_at(j, TILE)
            unit[tower, :, cols] = dot_nn(feat[...], weight[:, cols])
            return carry

        lax.fori_loop(0, WIDTH // TILE, column, 0)

        def scale(i, carry):
            rows = tile_at(i, STEP)
            value = unit[tower, rows, :]
            norm = jnp.sqrt(jnp.sum(value * value, axis=-1, keepdims=True) + 1e-06)
            value = value / norm
            unit[tower, rows, :] = value
            length[tower, rows, :] = jnp.broadcast_to(norm, (STEP, 128))
            store(rows, value.astype(BF))
            return carry

        lax.fori_loop(0, ROWS // STEP, scale, 0)

    def store_audio(rows, value):
        audio[0, rows, :] = value

    def store_score(rows, value):
        score[0, rows, :] = value

    def gather_copy(way, hop, chunk):
        first, count = chunk
        rows = pl.ds(first, count)
        if way == PLUS:
            here, there = (8 - (hop - 1)) % 8, 8 - hop
        else:
            here, there = hop - 1, hop
        index = CHUNKS.index(chunk)
        return remote(
            audio.at[here, rows], audio.at[there, rows],
            gather_send.at[way, hop - 1, index], gather_recv.at[way, hop - 1, index],
            device(dz=1 if way == PLUS else 7),
        )

    def ring_slot(way, ahead):
        return ahead if way == PLUS else (8 - ahead) % 8

    def ring_copy(way, hop, chunk):
        first, count = chunk
        rows = pl.ds(first, count)
        start = 0 if chunk in SUM_FAR[way] else 1
        src = part.at[ring_slot(way, 4 - hop), rows] if hop == start else ring.at[way, hop - 1, rows]
        index = CHUNKS.index(chunk)
        return remote(
            src, ring.at[way, hop, rows],
            ring_send.at[way, hop, index], ring_recv.at[way, hop, index],
            device(dz=1 if way == PLUS else 7),
        )

    def ring_take(way, hop, chunk):
        ring_copy(way, hop, chunk).wait_recv()
        if hop < 3:
            slot = ring_slot(way, 3 - hop)

            def add(rows):
                ring[way, hop, rows, :] = (
                    ring[way, hop, rows, :].astype(F32) + part[slot, rows, :].astype(F32)
                ).astype(BF)

            rows_in(chunk[0], chunk[1], add)
            launch(ring_copy(way, hop + 1, chunk))

    def tile_grads(slot, own):
        for side in range(2):
            logits = temper * dot_nt(audio[slot], score[side]) + bias
            grads = jax.nn.sigmoid(logits)
            if own and side == 0:
                row_ids = lax.broadcasted_iota(jnp.int32, (ROWS, ROWS), 0)
                col_ids = lax.broadcasted_iota(jnp.int32, (ROWS, ROWS), 1)
                grads = grads - (row_ids == col_ids).astype(F32)
            grad_t[side, slot] = grads.astype(BF)

        def column(j, carry):
            cols = tile_at(j, TILE)
            part[slot, :, cols] = (
                dot_nn(grad_t[0, slot], score[0, :, cols]) + dot_nn(grad_t[1, slot], score[1, :, cols])
            ).astype(BF)
            return carry

        lax.fori_loop(0, WIDTH // TILE, column, 0)

    def tile_pair(hop):
        def one(i, carry):
            tile_grads(hop + i * (8 - 2 * hop), False)
            return carry

        lax.fori_loop(0, 2, one, 0)

    def score_grad(side, store):
        def column(j, carry):
            cols = tile_at(j, TILE)
            total = dot_tn(grad_t[side, 0], audio[0, :, cols])
            for slot in range(1, 8):
                total += dot_tn(grad_t[side, slot], audio[slot, :, cols])
            store(cols, total)
            return carry

        lax.fori_loop(0, WIDTH // TILE, column, 0)

    def unit_grad(tower, value_of):
        def step(i, carry):
            rows = pl.ds(pl.multiple_of(i * 16, 16), 16)
            grad = factor * value_of(rows)
            vec = unit[tower, rows, :]
            radial = jnp.sum(vec * grad, axis=-1, keepdims=True)
            norm = length[tower, rows, 0:1]
            proj_grad[tower, rows, :] = ((grad - vec * radial) / norm).astype(BF)
            return carry

        lax.fori_loop(0, ROWS // 16, step, 0)

    def back(tower, weight, out):
        def column(j, carry):
            cols = tile_at(j, TILE)
            out[:, cols] = dot_nt(proj_grad[tower], weight[cols, :]).astype(BF)
            return carry

        lax.fori_loop(0, WIDTH // TILE, column, 0)

    def weight_part(tower, feat, owner):
        def step(z, carry):
            for j in range(2):
                cols = pl.ds(pl.multiple_of(owner * 512 + j * 256, 256), 256)
                value = dot_tn(feat[:, tile_at(z, 128)], proj_grad[tower, :, cols]).astype(BF)
                for q in range(2):
                    for x in range(4):
                        for route in range(2):
                            first = x * 32 + route * 16
                            outer[tower, owner * 4 + j * 2 + q, route, x, z] = value[
                                first : first + 16, q * 128 : q * 128 + 128
                            ]
            return carry

        lax.fori_loop(0, 8, step, 0)

    def core_copy(tower):
        other = lax.rem(core + 1, 2)
        return remote(
            outer.at[tower, pl.ds(other * 4, 4)], core_in.at[tower],
            core_send.at[tower], core_recv.at[tower], device(dc=1),
        )

    def one_copies(tower):
        copies = []
        for k in (2, 1, 3):
            copies.append(remote(
                half.at[tower, lax.rem(yy + k, 4), 0], y_in.at[tower, k - 1],
                one_send.at[tower, 0, k - 1], one_recv.at[tower, 0, k - 1], device(dy=k),
            ))
            copies.append(remote(
                half.at[tower, :, 1, lax.rem(xx + k, 4)], x_in.at[tower, k - 1],
                one_send.at[tower, 1, k - 1], one_recv.at[tower, 1, k - 1], device(dx=k),
            ))
        return copies

    def two_copies(tower):
        copies = []
        for k in (2, 1, 3):
            copies.append(remote(
                y_sum.at[tower, lax.rem(xx + k, 4)], x_in2.at[tower, k - 1],
                two_send.at[tower, 0, k - 1], two_recv.at[tower, 0, k - 1], device(dx=k),
            ))
            copies.append(remote(
                x_sum.at[tower, lax.rem(yy + k, 4)], y_in2.at[tower, k - 1],
                two_send.at[tower, 1, k - 1], two_recv.at[tower, 1, k - 1], device(dy=k),
            ))
        return copies

    def z_copies(tower):
        return [
            remote(
                z_out.at[tower, lax.rem(zz + k, 8)], z_in.at[tower, k - 1],
                z_send.at[tower, k - 1], z_recv.at[tower, k - 1], device(dz=k),
            )
            for k in (4, 3, 5, 2, 6, 1, 7)
        ]

    place_q = core * 4 + yy

    def all_copies(tower):
        return [
            remote(
                done.at[tower, place_q, xl], done.at[tower, place_q, xl],
                all_send.at[tower, k - 1], all_recv.at[tower, k - 1], flat_dp(k),
            )
            for k in range(1, 16)
        ]

    def stage_core_sum(tower):
        core_copy(tower).wait_recv()

        def step(i, carry):
            y = i // 4
            x = lax.rem(i, 4)
            for route in range(2):
                half[tower, y, route, x] = (
                    outer[tower, core * 4 + y, route, x].astype(F32) + core_in[tower, y, route, x].astype(F32)
                ).astype(BF)
            return carry

        lax.fori_loop(0, 16, step, 0)
        for copy in one_copies(tower):
            launch(copy)

    def stage_one_sum(tower):
        for copy in one_copies(tower):
            copy.wait_recv()

        def step(i, carry):
            total = half[tower, yy, 0, i].astype(F32)
            for k in range(3):
                total += y_in[tower, k, i].astype(F32)
            y_sum[tower, i] = total.astype(BF)
            total = half[tower, i, 1, xx].astype(F32)
            for k in range(3):
                total += x_in[tower, k, i].astype(F32)
            x_sum[tower, i] = total.astype(BF)
            return carry

        lax.fori_loop(0, 4, step, 0)
        for copy in two_copies(tower):
            launch(copy)

    def stage_two_sum(tower):
        for copy in two_copies(tower):
            copy.wait_recv()
        total = y_sum[tower, xx].astype(F32)
        for k in range(3):
            total += x_in2[tower, k].astype(F32)
        z_out[tower, :, 0] = total.astype(BF)
        total = x_sum[tower, yy].astype(F32)
        for k in range(3):
            total += y_in2[tower, k].astype(F32)
        z_out[tower, :, 1] = total.astype(BF)
        for copy in z_copies(tower):
            launch(copy)

    def stage_z_sum(tower):
        for copy in z_copies(tower):
            copy.wait_recv()
        total = z_out[tower, zz].astype(F32)
        for k in range(7):
            total += z_in[tower, k].astype(F32)
        done[tower, place_q, xl] = total.astype(BF)
        for copy in all_copies(tower):
            launch(copy)

    def stage_all(tower, out):
        for copy in all_copies(tower):
            copy.wait_recv()
        for q in range(8):
            for half_rows in range(2):
                for route in range(2):
                    first = half_rows * 32 + route * 16
                    out[first : first + 16, q * 128 : q * 128 + 128] = done[tower, q, half_rows, route]

    project(1, feat_a, weight_a, store_audio)
    pl.semaphore_wait(barrier, len(peers))
    for chunk in CHUNKS:
        for way in (PLUS, MINUS):
            launch(gather_copy(way, 1, chunk))
    project(0, feat_s, weight_s, store_score)
    pair = remote(score.at[0], score.at[1], side_send.at[0], side_recv.at[0], device(dx=2))
    launch(pair)

    for hop in range(1, 5):
        for chunk in CHUNKS:
            for way in (PLUS, MINUS):
                if hop == 4 and chunk not in GATHER_FAR[way]:
                    continue
                gather_copy(way, hop, chunk).wait_recv()
                if hop < 3 or (hop == 3 and chunk in GATHER_FAR[way]):
                    launch(gather_copy(way, hop + 1, chunk))
        if hop == 1:
            pair.wait_recv()
            tile_grads(0, True)
        if hop < 4:
            tile_pair(hop)
        else:
            tile_grads(4, False)
        if hop >= 3:
            for way in (PLUS, MINUS):
                for chunk in SUM_FAR[way] if hop == 4 else SUM_FAR[1 - way]:
                    launch(ring_copy(way, 4 - hop, chunk))

    def store_side(cols, value):
        side_out[:, cols] = value.astype(BF)

    def store_own(cols, value):
        emb_grad[:, cols] = value

    def near(hop):
        for k in range(2):
            for way in (PLUS, MINUS):
                ring_take(way, hop, SUM_FAR[1 - way][k])

    def far(hop):
        for k in range(2):
            for way in (PLUS, MINUS):
                ring_take(way, hop, SUM_FAR[way][k])

    score_grad(1, store_side)
    side = remote(side_out, side_in, side_send.at[1], side_recv.at[1], device(dx=2))
    launch(side)
    near(1)
    score_grad(0, store_own)
    far(0)
    near(2)
    side.wait_recv()
    unit_grad(0, lambda rows: emb_grad[rows, :] + side_in[rows, :].astype(F32))
    weight_part(0, feat_s, lax.rem(core + 1, 2))
    launch(core_copy(0))
    far(1)
    weight_part(0, feat_s, core)
    stage_core_sum(0)
    back(0, weight_s, back_s)
    near(3)
    far(2)
    stage_one_sum(0)
    stage_two_sum(0)
    far(3)

    def audio_value(rows):
        return (
            part[0, rows, :].astype(F32) + ring[PLUS, 3, rows, :].astype(F32) + ring[MINUS, 3, rows, :].astype(F32)
        )

    unit_grad(1, audio_value)
    weight_part(1, feat_a, lax.rem(core + 1, 2))
    launch(core_copy(1))
    weight_part(1, feat_a, core)
    stage_core_sum(1)
    back(1, weight_a, back_a)
    stage_z_sum(0)
    stage_one_sum(1)
    stage_all(0, rows_s)
    stage_two_sum(1)
    stage_z_sum(1)
    stage_all(1, rows_a)
    for copy in pending:
        copy.wait_send()


def body(score_feats, audio_feats, score_weight, audio_weight, log_temp, logit_bias, loss_scale):
    groups_rows = float(lax.axis_size("dp") * lax.axis_size("blk") * score_feats.shape[1])
    vmem = pl.BlockSpec(memory_space=pltpu.VMEM)
    smem = pl.BlockSpec(memory_space=pltpu.SMEM)
    rows = jax.ShapeDtypeStruct((ROWS, WIDTH), BF)
    sums = jax.ShapeDtypeStruct((64, WIDTH), BF)
    dma = pltpu.SemaphoreType.DMA
    scratch = [
        pltpu.VMEM((2, ROWS, WIDTH), F32),
        pltpu.VMEM((2, ROWS, 128), F32),
        pltpu.VMEM((8, ROWS, WIDTH), BF),
        pltpu.VMEM((2, ROWS, WIDTH), BF),
        pltpu.VMEM((2, 8, ROWS, ROWS), BF),
        pltpu.VMEM((8, ROWS, WIDTH), BF),
        pltpu.VMEM((2, 4, ROWS, WIDTH), BF),
        pltpu.VMEM((ROWS, WIDTH), BF),
        pltpu.VMEM((ROWS, WIDTH), BF),
        pltpu.VMEM((ROWS, WIDTH), F32),
        pltpu.VMEM((2, ROWS, WIDTH), BF),
        pltpu.VMEM((2, 8, 2, 4, 8, 16, 128), BF),
        pltpu.VMEM((2, 4, 2, 4, 8, 16, 128), BF),
        pltpu.VMEM((2, 4, 2, 4, 8, 16, 128), BF),
        pltpu.VMEM((2, 3, 4, 8, 16, 128), BF),
        pltpu.VMEM((2, 3, 4, 8, 16, 128), BF),
        pltpu.VMEM((2, 4, 8, 16, 128), BF),
        pltpu.VMEM((2, 4, 8, 16, 128), BF),
        pltpu.VMEM((2, 3, 8, 16, 128), BF),
        pltpu.VMEM((2, 3, 8, 16, 128), BF),
        pltpu.VMEM((2, 8, 2, 16, 128), BF),
        pltpu.VMEM((2, 7, 2, 16, 128), BF),
        pltpu.VMEM((2, 8, 2, 2, 16, 128), BF),
        dma((2, 4, 4)),
        dma((2, 4, 4)),
        dma((2, 4, 4)),
        dma((2, 4, 4)),
        dma((2,)),
        dma((2,)),
        dma((2,)),
        dma((2,)),
        dma((2, 2, 3)),
        dma((2, 2, 3)),
        dma((2, 2, 3)),
        dma((2, 2, 3)),
        dma((2, 7)),
        dma((2, 7)),
        dma((2, 15)),
        dma((2, 15)),
    ]
    back_s, back_a, rows_s, rows_a = pl.pallas_call(
        functools.partial(kernel, groups_rows),
        out_shape=(rows, rows, sums, sums),
        in_specs=[vmem] * 4 + [smem] * 3,
        out_specs=(vmem,) * 4,
        scratch_shapes=scratch,
        compiler_params=pltpu.CompilerParams(
            collective_id=0, has_side_effects=True, vmem_limit_bytes=58 * 2**20
        ),
    )(score_feats[0], audio_feats[0], score_weight, audio_weight, log_temp, logit_bias, loss_scale)
    return back_s[None], back_a[None], rows_s.astype(F32), rows_a.astype(F32)


def solution(mesh):
    in_specs = (P("dp", "blk", None), P("dp", "blk", None), P(), P(), P(), P(), P())
    out_specs = (P("dp", "blk", None), P("dp", "blk", None), P("blk", None), P("blk", None))
    return jax.shard_map(body, mesh=mesh, in_specs=in_specs, out_specs=out_specs, check_vma=False)
```

time: 740 us -> 129 us (0.17)
  waiting for transfers between devices: 669 us -> 0 us
  Pallas kernels: 0 us -> 121 us
  matrix products: 34.1 us -> 0 us
  between operations: 15.9 us -> 2.59 us
  local copies, waits for them, and re-layouts: 15.3 us -> 2.62 us
    reduce_scatter x1 -> x0, waiting for transfers between devices: 209 us -> none  [body(): lax.psum_scatter(jnp.dot(logit_grad.T, score_emb, preferred_element_type=...]
    unnamed x5 -> x0, waiting for transfers between devices: 207 us -> none
    all_gather x1 -> x0, waiting for transfers between devices: 130 us -> none  [body(): gathered = lax.all_gather(audio_emb, 'blk', axis=0, tiled=True)]
    psum x1 -> x0, waiting for transfers between devices: 123 us -> none  [body(): summed = lax.psum(reduced, 'dp').astype(jnp.float32)]
    pallas_call x0 -> x1, Pallas kernels: none -> 121 us  [body(): pl.pallas_call(functools.partial(kernel, groups_rows), out_shape=(rows, r...]
    dot_general x9 -> x0, matrix products: 34.1 us -> none  [the longest x1 6.88 us: logit_tile(): jnp.dot(left_emb, right_emb.T, preferred_element_type=jnp.float32)]
    unnamed x18 -> x4, local copies, waits for them, and re-layouts: 13.4 us -> 2.62 us
  transfers between devices with their start and end apart: 4 -> 0, of which waited for: 4 -> 0; matrix products, arithmetic and copies ran while one was open for 2% -> 0% of each run, Pallas kernels for 0% -> 0%
where the time goes in v1:
time: 129 us
  Pallas kernels  121 us (94%)
  other arithmetic  3.3 us (3%)
  local copies, waits for them, and re-layouts  2.62 us (2%)
  between operations  2.59 us (2%)
    pallas_call x1, Pallas kernels, body(): pl.pallas_call(functools.partial(kernel, groups_rows), out_shape=(rows, r...  121 us
    convert_element_type x2, other arithmetic, body(): return (back_s[None], back_a[None], rows_s.astype(F32), rows_a.astype(F32))  3.3 us
    unnamed x4, local copies, waits for them, and re-layouts  2.62 us

profile of v1, /device:TPU:1, one launch (start us, length us, event | category | flops | bytes accessed | tf_op | source)
XLA Modules:
  0.0 129.2 jit_solution(11245545218158277452)
XLA Ops:
  2.6 120.6 %shard_map.102 = (bf16[240,1024]{1,0:T(8,128)(2,1)}, bf16[240,1024]{1,0:T(8,128)(2,1)}, bf16[64,1024]{1,0:T(8,128)(2,1)}, bf16[64,1024]{1,0:T(8,128)(2,1)}) custom-call(bf16[240,1024]{1,0:T(8,128)(2,1)} %bitcast.4, bf16[240,1024]{1,0:T(8,128)(2,1)} %bitcast.5, bf16[1024,1024]{1,0:T(8,128)(2,1)} %weight_s.1, bf16[1024,1024]{1,0:T(8,128)(2,1)} %weight_a.1, ...), custom_call_target="tpu_custom_call" | custom-call | tf_op jit(solution)/shard_map/pallas_call | solution.py:491
  123.2 0.0 copy-start
  123.2 1.7 %convert_element_type.6 = f32[64,1024]{1,0:T(8,128)} convert(bf16[64,1024]{1,0:T(8,128)(2,1)} %get-tuple-element.10) | non-fusion elementwise | flops 65536 | bytes 393216 | tf_op jit(solution)/shard_map/convert_element_type | solution.py:501
  124.9 1.6 %convert_element_type.7 = f32[64,1024]{1,0:T(8,128)} convert(bf16[64,1024]{1,0:T(8,128)(2,1)} %get-tuple-element.11) | non-fusion elementwise | flops 65536 | bytes 393216 | tf_op jit(solution)/shard_map/convert_element_type | solution.py:501
  126.5 1.8 %copy.16 = bf16[1,240,1024]{2,1,0:T(8,128)(2,1)} copy(bf16[1,240,1024]{2,1,0:T(8,128)(2,1)} %bitcast.7) | data formatting | bytes 983040
  128.4 0.0 copy-done
  128.4 0.8 copy.17
Async XLA Ops:
  123.2 5.2 %copy-start = (bf16[240,1024]{1,0:T(8,128)(2,1)S(1)}, bf16[240,1024]{1,0:T(8,128)(2,1)}, u32[]{:S(2)}) copy-start(bf16[240,1024]{1,0:T(8,128)(2,1)} %get-tuple-element.9) | copy-start | bytes 1474564

commit v2 on v1

--- a/solution.py
+++ b/solution.py
@@ -41,8 +41,11 @@
 
 def kernel(
     groups_rows,
+    feat_s_in, feat_a_in, weight_s_in, weight_a_in, temp_in, bias_in, scale_in,
+    back_s_out, back_a_out, rows_s_out, rows_a_out,
     feat_s, feat_a, weight_s, weight_a, temp_ref, bias_ref, scale_ref,
-    back_s, back_a, rows_s, rows_a,
+    back_s, back_a, rows_s, rows_a, feat_t,
+    load_sem, save_sem,
     unit, length, audio, score, grad_t, part, ring, side_out, side_in, emb_grad, proj_grad,
     outer, core_in, half, y_in, x_in, y_sum, x_sum, x_in2, y_in2, z_out, z_in, done,
     gather_send, gather_recv, ring_send, ring_recv, side_send, side_recv,
@@ -74,15 +77,28 @@
     for peer in peers:
         pl.semaphore_signal(barrier, inc=1, device_id=peer, device_id_type=MESH)
 
+    loads = [
+        pltpu.make_async_copy(src, dst, load_sem.at[i])
+        for i, (src, dst) in enumerate((
+            (feat_a_in, feat_a), (weight_a_in, weight_a), (feat_s_in, feat_s), (weight_s_in, weight_s),
+            (temp_in, temp_ref), (bias_in, bias_ref), (scale_in, scale_ref),
+        ))
+    ]
+    for copy in loads:
+        copy.start()
+    for copy in loads[4:]:
+        copy.wait()
+
     temper = jnp.exp(jnp.full((1, 1), temp_ref[0], F32))
     bias = bias_ref[0]
     factor = scale_ref[0] * temper / groups_rows
 
-    pending = []
-
     def launch(copy):
         copy.start()
-        pending.append(copy)
+
+    def launch_all(copies):
+        for copy in copies:
+            copy.start()
 
     def rows_in(first, count, fn):
         def step(i, carry):
@@ -127,7 +143,7 @@
         index = CHUNKS.index(chunk)
         return remote(
             audio.at[here, rows], audio.at[there, rows],
-            gather_send.at[way, hop - 1, index], gather_recv.at[way, hop - 1, index],
+            gather_send.at[way, hop - 1], gather_recv.at[way, hop - 1, index],
             device(dz=1 if way == PLUS else 7),
         )
 
@@ -142,7 +158,7 @@
         index = CHUNKS.index(chunk)
         return remote(
             src, ring.at[way, hop, rows],
-            ring_send.at[way, hop, index], ring_recv.at[way, hop, index],
+            ring_send.at[way, hop], ring_recv.at[way, hop, index],
             device(dz=1 if way == PLUS else 7),
         )
 
@@ -196,17 +212,15 @@
 
         lax.fori_loop(0, WIDTH // TILE, column, 0)
 
-    def unit_grad(tower, value_of):
-        def step(i, carry):
-            rows = pl.ds(pl.multiple_of(i * 16, 16), 16)
+    def unit_grad(tower, value_of, first, count):
+        def step(rows):
             grad = factor * value_of(rows)
             vec = unit[tower, rows, :]
             radial = jnp.sum(vec * grad, axis=-1, keepdims=True)
             norm = length[tower, rows, 0:1]
             proj_grad[tower, rows, :] = ((grad - vec * radial) / norm).astype(BF)
-            return carry
-
-        lax.fori_loop(0, ROWS // 16, step, 0)
+
+        rows_in(first, count, step)
 
     def back(tower, weight, out):
         def column(j, carry):
@@ -216,39 +230,61 @@
 
         lax.fori_loop(0, WIDTH // TILE, column, 0)
 
-    def weight_part(tower, feat, owner):
+    def transpose(tower, feat):
         def step(z, carry):
-            for j in range(2):
-                cols = pl.ds(pl.multiple_of(owner * 512 + j * 256, 256), 256)
-                value = dot_tn(feat[:, tile_at(z, 128)], proj_grad[tower, :, cols]).astype(BF)
-                for q in range(2):
-                    for x in range(4):
-                        for route in range(2):
-                            first = x * 32 + route * 16
-                            outer[tower, owner * 4 + j * 2 + q, route, x, z] = value[
-                                first : first + 16, q * 128 : q * 128 + 128
-                            ]
+            cols = tile_at(z, 128)
+            feat_t[tower, cols, :] = feat[:, cols].T
             return carry
 
         lax.fori_loop(0, 8, step, 0)
 
-    def core_copy(tower):
+    def core_pair(order):
+        return lax.rem(yy // 2 + 1 + order, 2)
+
+    def weight_part(tower, owner, order):
+        pair = core_pair(order)
+        cols = tile_at(owner * 2 + pair, 256)
+
+        def step(z, carry):
+            value = dot_nn(feat_t[tower, tile_at(z, 128), :], proj_grad[tower, :, cols]).astype(BF)
+            for q in range(2):
+                for x in range(4):
+                    for route in range(2):
+                        first = x * 32 + route * 16
+                        outer[tower, owner * 4 + pair * 2 + q, route, x, z] = value[
+                            first : first + 16, q * 128 : q * 128 + 128
+                        ]
+            return carry
+
+        lax.fori_loop(0, 8, step, 0)
+
+    def core_copy(tower, order):
         other = lax.rem(core + 1, 2)
+        pair = core_pair(order)
         return remote(
-            outer.at[tower, pl.ds(other * 4, 4)], core_in.at[tower],
-            core_send.at[tower], core_recv.at[tower], device(dc=1),
+            outer.at[tower, pl.ds(other * 4 + pair * 2, 2)], core_in.at[tower, pl.ds(pair * 2, 2)],
+            core_send.at[tower, order], core_recv.at[tower, order], device(dc=1),
         )
+
+    def weight_other(tower):
+        for order in range(2):
+            weight_part(tower, lax.rem(core + 1, 2), order)
+            launch(core_copy(tower, order))
+
+    def weight_own(tower):
+        for order in range(2):
+            weight_part(tower, core, order)
 
     def one_copies(tower):
         copies = []
         for k in (2, 1, 3):
             copies.append(remote(
                 half.at[tower, lax.rem(yy + k, 4), 0], y_in.at[tower, k - 1],
-                one_send.at[tower, 0, k - 1], one_recv.at[tower, 0, k - 1], device(dy=k),
+                one_send.at[tower, 0], one_recv.at[tower, 0], device(dy=k),
             ))
             copies.append(remote(
                 half.at[tower, :, 1, lax.rem(xx + k, 4)], x_in.at[tower, k - 1],
-                one_send.at[tower, 1, k - 1], one_recv.at[tower, 1, k - 1], device(dx=k),
+                one_send.at[tower, 1], one_recv.at[tower, 1], device(dx=k),
             ))
         return copies
 
@@ -257,11 +293,11 @@
         for k in (2, 1, 3):
             copies.append(remote(
                 y_sum.at[tower, lax.rem(xx + k, 4)], x_in2.at[tower, k - 1],
-                two_send.at[tower, 0, k - 1], two_recv.at[tower, 0, k - 1], device(dx=k),
+                two_send.at[tower, 0], two_recv.at[tower, 0], device(dx=k),
             ))
             copies.append(remote(
                 x_sum.at[tower, lax.rem(yy + k, 4)], y_in2.at[tower, k - 1],
-                two_send.at[tower, 1, k - 1], two_recv.at[tower, 1, k - 1], device(dy=k),
+                two_send.at[tower, 1], two_recv.at[tower, 1], device(dy=k),
             ))
         return copies
 
@@ -269,27 +305,41 @@
         return [
             remote(
                 z_out.at[tower, lax.rem(zz + k, 8)], z_in.at[tower, k - 1],
-                z_send.at[tower, k - 1], z_recv.at[tower, k - 1], device(dz=k),
+                z_send.at[tower, 0], z_recv.at[tower, 0], device(dz=k),
             )
             for k in (4, 3, 5, 2, 6, 1, 7)
         ]
 
-    place_q = core * 4 + yy
+    place = (core * 4 + yy) * 2 + xl
 
     def all_copies(tower):
         return [
             remote(
-                done.at[tower, place_q, xl], done.at[tower, place_q, xl],
-                all_send.at[tower, k - 1], all_recv.at[tower, k - 1], flat_dp(k),
+                done.at[tower, place], done.at[tower, place],
+                all_send.at[tower, 0], all_recv.at[tower, 0], flat_dp(k),
             )
             for k in range(1, 16)
         ]
 
-    def stage_core_sum(tower):
-        core_copy(tower).wait_recv()
+    def stage_waits(tower, name):
+        bufs, send, recv = {
+            "one": ((y_in, x_in), one_send, one_recv),
+            "two": ((x_in2, y_in2), two_send, two_recv),
+            "z": ((z_in,), z_send, z_recv),
+            "all": ((done,), all_send, all_recv),
+        }[name]
+        copies = []
+        for i, buf in enumerate(bufs):
+            view = buf.at[tower, pl.ds(0, 15)] if name == "all" else buf.at[tower]
+            copies.append(remote(view, view, send.at[tower, i], recv.at[tower, i], device(dc=1)))
+        return copies
+
+    def stage_core_sum(tower, order):
+        pair = core_pair(order)
+        core_copy(tower, order).wait_recv()
 
         def step(i, carry):
-            y = i // 4
+            y = pair * 2 + i // 4
             x = lax.rem(i, 4)
             for route in range(2):
                 half[tower, y, route, x] = (
@@ -297,12 +347,12 @@
                 ).astype(BF)
             return carry
 
-        lax.fori_loop(0, 16, step, 0)
-        for copy in one_copies(tower):
-            launch(copy)
+        lax.fori_loop(0, 8, step, 0)
+        if order == 1:
+            launch_all(one_copies(tower))
 
     def stage_one_sum(tower):
-        for copy in one_copies(tower):
+        for copy in stage_waits(tower, "one"):
             copy.wait_recv()
 
         def step(i, carry):
@@ -317,11 +367,10 @@
             return carry
 
         lax.fori_loop(0, 4, step, 0)
-        for copy in two_copies(tower):
-            launch(copy)
+        launch_all(two_copies(tower))
 
     def stage_two_sum(tower):
-        for copy in two_copies(tower):
+        for copy in stage_waits(tower, "two"):
             copy.wait_recv()
         total = y_sum[tower, xx].astype(F32)
         for k in range(3):
@@ -331,36 +380,40 @@
         for k in range(3):
             total += y_in2[tower, k].astype(F32)
         z_out[tower, :, 1] = total.astype(BF)
-        for copy in z_copies(tower):
-            launch(copy)
+        launch_all(z_copies(tower))
 
     def stage_z_sum(tower):
-        for copy in z_copies(tower):
+        for copy in stage_waits(tower, "z"):
             copy.wait_recv()
         total = z_out[tower, zz].astype(F32)
         for k in range(7):
             total += z_in[tower, k].astype(F32)
-        done[tower, place_q, xl] = total.astype(BF)
-        for copy in all_copies(tower):
-            launch(copy)
+        done[tower, place] = total.astype(BF)
+        launch_all(all_copies(tower))
 
     def stage_all(tower, out):
-        for copy in all_copies(tower):
+        for copy in stage_waits(tower, "all"):
             copy.wait_recv()
         for q in range(8):
             for half_rows in range(2):
                 for route in range(2):
                     first = half_rows * 32 + route * 16
-                    out[first : first + 16, q * 128 : q * 128 + 128] = done[tower, q, half_rows, route]
-
+                    out[first : first + 16, q * 128 : q * 128 + 128] = done[tower, q * 2 + half_rows, route].astype(F32)
+
+    loads[0].wait()
+    loads[1].wait()
     project(1, feat_a, weight_a, store_audio)
     pl.semaphore_wait(barrier, len(peers))
     for chunk in CHUNKS:
         for way in (PLUS, MINUS):
             launch(gather_copy(way, 1, chunk))
+    loads[2].wait()
+    loads[3].wait()
     project(0, feat_s, weight_s, store_score)
     pair = remote(score.at[0], score.at[1], side_send.at[0], side_recv.at[0], device(dx=2))
     launch(pair)
+    transpose(0, feat_s)
+    transpose(1, feat_a)
 
     for hop in range(1, 5):
         for chunk in CHUNKS:
@@ -406,48 +459,104 @@
     far(0)
     near(2)
     side.wait_recv()
-    unit_grad(0, lambda rows: emb_grad[rows, :] + side_in[rows, :].astype(F32))
-    weight_part(0, feat_s, lax.rem(core + 1, 2))
-    launch(core_copy(0))
+    unit_grad(0, lambda rows: emb_grad[rows, :] + side_in[rows, :].astype(F32), 0, ROWS)
+    weight_other(0)
     far(1)
-    weight_part(0, feat_s, core)
-    stage_core_sum(0)
+    weight_own(0)
+    stage_core_sum(0, 0)
+    stage_core_sum(0, 1)
     back(0, weight_s, back_s)
+    saves = [
+        pltpu.make_async_copy(src, dst, save_sem.at[i])
+        for i, (src, dst) in enumerate(
+            ((back_s, back_s_out), (back_a, back_a_out), (rows_s, rows_s_out), (rows_a, rows_a_out))
+        )
+    ]
+    saves[0].start()
     near(3)
     far(2)
     stage_one_sum(0)
     stage_two_sum(0)
-    far(3)
 
     def audio_value(rows):
         return (
             part[0, rows, :].astype(F32) + ring[PLUS, 3, rows, :].astype(F32) + ring[MINUS, 3, rows, :].astype(F32)
         )
 
-    unit_grad(1, audio_value)
-    weight_part(1, feat_a, lax.rem(core + 1, 2))
-    launch(core_copy(1))
-    weight_part(1, feat_a, core)
-    stage_core_sum(1)
+    for k in range(2):
+        for way in (PLUS, MINUS):
+            ring_take(way, 3, SUM_FAR[way][k])
+            unit_grad(1, audio_value, *SUM_FAR[way][k])
+    weight_other(1)
+    weight_own(1)
+    stage_core_sum(1, 0)
+    stage_core_sum(1, 1)
     back(1, weight_a, back_a)
+    saves[1].start()
     stage_z_sum(0)
     stage_one_sum(1)
     stage_all(0, rows_s)
+    saves[2].start()
     stage_two_sum(1)
     stage_z_sum(1)
     stage_all(1, rows_a)
-    for copy in pending:
-        copy.wait_send()
+    saves[3].start()
+
+    for way in (PLUS, MINUS):
+        for hop in range(4):
+            for kind in range(2):
+                far_rows = (GATHER_FAR, SUM_FAR)[kind][way]
+                edge = hop == (3, 0)[kind]
+                rows = pl.ds(far_rows[0][0], far_rows[0][1] + far_rows[1][1]) if edge else pl.ds(0, ROWS)
+                buf = (audio.at[1, rows], ring.at[way, 1, rows])[kind]
+                sem = (gather_send, ring_send)[kind].at[way, hop]
+                remote(buf, buf, sem, (gather_recv, ring_recv)[kind].at[way, hop, 0], device(dz=1)).wait_send()
+    pair.wait_send()
+    side.wait_send()
+    for tower in range(2):
+        for order in range(2):
+            core_copy(tower, order).wait_send()
+        for name in ("one", "two", "z", "all"):
+            for copy in stage_waits(tower, name):
+                copy.wait_send()
+    for copy in saves:
+        copy.wait()
+
+
+def finish(*refs):
+    sources, targets, held, load, save = refs[:4], refs[4:8], refs[8:12], refs[12], refs[13]
+    loads = [pltpu.make_async_copy(sources[i], held[i], load.at[i]) for i in range(4)]
+    saves = [pltpu.make_async_copy(held[i], targets[i], save.at[i]) for i in range(4)]
+    for copy in loads:
+        copy.start()
+    for i in range(4):
+        loads[i].wait()
+        saves[i].start()
+    for copy in saves:
+        copy.wait()
 
 
 def body(score_feats, audio_feats, score_weight, audio_weight, log_temp, logit_bias, loss_scale):
     groups_rows = float(lax.axis_size("dp") * lax.axis_size("blk") * score_feats.shape[1])
-    vmem = pl.BlockSpec(memory_space=pltpu.VMEM)
-    smem = pl.BlockSpec(memory_space=pltpu.SMEM)
+    anywhere = pl.BlockSpec(memory_space=pl.ANY)
     rows = jax.ShapeDtypeStruct((ROWS, WIDTH), BF)
-    sums = jax.ShapeDtypeStruct((64, WIDTH), BF)
+    sums = jax.ShapeDtypeStruct((64, WIDTH), F32)
     dma = pltpu.SemaphoreType.DMA
     scratch = [
+        pltpu.VMEM((ROWS, WIDTH), BF),
+        pltpu.VMEM((ROWS, WIDTH), BF),
+        pltpu.VMEM((WIDTH, WIDTH), BF),
+        pltpu.VMEM((WIDTH, WIDTH), BF),
+        pltpu.SMEM((1,), F32),
+        pltpu.SMEM((1,), F32),
+        pltpu.SMEM((1,), F32),
+        pltpu.VMEM((ROWS, WIDTH), BF),
+        pltpu.VMEM((ROWS, WIDTH), BF),
+        pltpu.VMEM((64, WIDTH), F32),
+        pltpu.VMEM((64, WIDTH), F32),
+        pltpu.VMEM((2, WIDTH, ROWS), BF),
+        dma((7,)),
+        dma((4,)),
         pltpu.VMEM((2, ROWS, WIDTH), F32),
         pltpu.VMEM((2, ROWS, 128), F32),
         pltpu.VMEM((8, ROWS, WIDTH), BF),
@@ -470,35 +579,43 @@
         pltpu.VMEM((2, 3, 8, 16, 128), BF),
         pltpu.VMEM((2, 8, 2, 16, 128), BF),
         pltpu.VMEM((2, 7, 2, 16, 128), BF),
-        pltpu.VMEM((2, 8, 2, 2, 16, 128), BF),
+        pltpu.VMEM((2, 16, 2, 16, 128), BF),
+        dma((2, 4)),
         dma((2, 4, 4)),
-        dma((2, 4, 4)),
-        dma((2, 4, 4)),
+        dma((2, 4)),
         dma((2, 4, 4)),
         dma((2,)),
         dma((2,)),
-        dma((2,)),
-        dma((2,)),
-        dma((2, 2, 3)),
-        dma((2, 2, 3)),
-        dma((2, 2, 3)),
-        dma((2, 2, 3)),
-        dma((2, 7)),
-        dma((2, 7)),
-        dma((2, 15)),
-        dma((2, 15)),
+        dma((2, 2)),
+        dma((2, 2)),
+        dma((2, 2)),
+        dma((2, 2)),
+        dma((2, 2)),
+        dma((2, 2)),
+        dma((2, 1)),
+        dma((2, 1)),
+        dma((2, 1)),
+        dma((2, 1)),
     ]
-    back_s, back_a, rows_s, rows_a = pl.pallas_call(
+    shapes = (rows, rows, sums, sums)
+    results = pl.pallas_call(
         functools.partial(kernel, groups_rows),
-        out_shape=(rows, rows, sums, sums),
-        in_specs=[vmem] * 4 + [smem] * 3,
-        out_specs=(vmem,) * 4,
+        out_shape=shapes,
+        in_specs=[anywhere] * 7,
+        out_specs=(anywhere,) * 4,
         scratch_shapes=scratch,
         compiler_params=pltpu.CompilerParams(
             collective_id=0, has_side_effects=True, vmem_limit_bytes=58 * 2**20
         ),
     )(score_feats[0], audio_feats[0], score_weight, audio_weight, log_temp, logit_bias, loss_scale)
-    return back_s[None], back_a[None], rows_s.astype(F32), rows_a.astype(F32)
+    back_s, back_a, rows_s, rows_a = pl.pallas_call(
+        finish,
+        out_shape=shapes,
+        in_specs=[anywhere] * 4,
+        out_specs=(anywhere,) * 4,
+        scratch_shapes=[pltpu.VMEM(v.shape, v.dtype) for v in shapes] + [dma((4,)), dma((4,))],
+    )(*results)
+    return back_s[None], back_a[None], rows_s, rows_a
 
 
 def solution(mesh):

time: 129 us -> 122 us (0.946)
  other arithmetic: 3.3 us -> 0 us
  local copies, waits for them, and re-layouts: 2.62 us -> 0 us
  Pallas kernels: 121 us -> 119 us
    convert_element_type x2 -> x0, other arithmetic: 3.3 us -> none  [body(): return (back_s[None], back_a[None], rows_s.astype(F32), rows_a.astype(F32))]
    unnamed x4 -> x0, local copies, waits for them, and re-layouts: 2.62 us -> none
    pallas_call x1 -> x2, Pallas kernels: 121 us -> 119 us  [the longest x1 117 us: body(): pl.pallas_call(functools.partial(kernel, groups_rows), out_shape=shapes,...]
where the time goes in v2:
time: 122 us; the launch traced here: 121 us
  Pallas kernels  119 us (98%)
  between operations  2.58 us (2%)
    pallas_call x1, Pallas kernels, body(): pl.pallas_call(functools.partial(kernel, groups_rows), out_shape=shapes,...  117 us

profile of v2, /device:TPU:1, one launch (start us, length us, event | category | flops | bytes accessed | tf_op | source)
XLA Modules:
  0.0 121.4 jit_solution(4761453169580852622)
XLA Ops:
  2.6 116.7 %shard_map.102 = (bf16[240,1024]{1,0:T(8,128)(2,1)}, bf16[240,1024]{1,0:T(8,128)(2,1)}, f32[64,1024]{1,0:T(8,128)}, f32[64,1024]{1,0:T(8,128)}) custom-call(bf16[240,1024]{1,0:T(8,128)(2,1)} %bitcast.4, bf16[240,1024]{1,0:T(8,128)(2,1)} %bitcast.5, bf16[1024,1024]{1,0:T(8,128)(2,1)} %weight_s_in.1, bf16[1024,1024]{1,0:T(8,128)(2,1)} %weight_a_in.1, ...), custom_call_target="tpu_custom_call" | custom-call | tf_op jit(solution)/shard_map/pallas_call | solution.py:601
  119.2 2.2 %shard_map.103 = (bf16[240,1024]{1,0:T(8,128)(2,1)}, bf16[240,1024]{1,0:T(8,128)(2,1)}, f32[64,1024]{1,0:T(8,128)}, f32[64,1024]{1,0:T(8,128)}) custom-call(bf16[240,1024]{1,0:T(8,128)(2,1)} %get-tuple-element.12.refs_0_, bf16[240,1024]{1,0:T(8,128)(2,1)} %get-tuple-element.13.refs_1_, f32[64,1024]{1,0:T(8,128)} %get-tuple-element.14.refs_2_, ...), custom_call_target="tpu_custom_call" | custom-call | tf_op jit(solution)/shard_map/pallas_call | solution.py:611

commit v3 on v2

--- a/solution.py
+++ b/solution.py
@@ -42,12 +42,11 @@
 def kernel(
     groups_rows,
     feat_s_in, feat_a_in, weight_s_in, weight_a_in, temp_in, bias_in, scale_in,
-    back_s_out, back_a_out, rows_s_out, rows_a_out,
-    feat_s, feat_a, weight_s, weight_a, temp_ref, bias_ref, scale_ref,
-    back_s, back_a, rows_s, rows_a, feat_t,
-    load_sem, save_sem,
+    back_s, back_a, rows_s, rows_a,
+    feat_s, feat_a, weight_s, weight_a, temp_ref, bias_ref, scale_ref, feat_t,
+    load_sem,
     unit, length, audio, score, grad_t, part, ring, side_out, side_in, emb_grad, proj_grad,
-    outer, core_in, half, y_in, x_in, y_sum, x_sum, x_in2, y_in2, z_out, z_in, done,
+    feat_other, proj_other, half, y_in, x_in, y_sum, x_sum, x_in2, y_in2, z_out, z_in, done,
     gather_send, gather_recv, ring_send, ring_recv, side_send, side_recv,
     core_send, core_recv, one_send, one_recv, two_send, two_recv, z_send, z_recv, all_send, all_recv,
 ):
@@ -201,7 +200,7 @@
 
         lax.fori_loop(0, 2, one, 0)
 
-    def score_grad(side, store):
+    def score_grad(side, store, first, count):
         def column(j, carry):
             cols = tile_at(j, TILE)
             total = dot_tn(grad_t[side, 0], audio[0, :, cols])
@@ -210,7 +209,7 @@
             store(cols, total)
             return carry
 
-        lax.fori_loop(0, WIDTH // TILE, column, 0)
+        lax.fori_loop(first, first + count, column, 0)
 
     def unit_grad(tower, value_of, first, count):
         def step(rows):
@@ -230,63 +229,66 @@
 
         lax.fori_loop(0, WIDTH // TILE, column, 0)
 
-    def transpose(tower, feat):
+    def transpose(tower, side, feat):
         def step(z, carry):
             cols = tile_at(z, 128)
-            feat_t[tower, cols, :] = feat[:, cols].T
+            feat_t[tower, side, cols, :] = feat[:, cols].T
             return carry
 
         lax.fori_loop(0, 8, step, 0)
 
-    def core_pair(order):
-        return lax.rem(yy // 2 + 1 + order, 2)
-
-    def weight_part(tower, owner, order):
-        pair = core_pair(order)
-        cols = tile_at(owner * 2 + pair, 256)
-
-        def step(z, carry):
-            value = dot_nn(feat_t[tower, tile_at(z, 128), :], proj_grad[tower, :, cols]).astype(BF)
-            for q in range(2):
-                for x in range(4):
-                    for route in range(2):
-                        first = x * 32 + route * 16
-                        outer[tower, owner * 4 + pair * 2 + q, route, x, z] = value[
-                            first : first + 16, q * 128 : q * 128 + 128
-                        ]
-            return carry
-
-        lax.fori_loop(0, 8, step, 0)
-
-    def core_copy(tower, order):
-        other = lax.rem(core + 1, 2)
-        pair = core_pair(order)
+    def feat_copy(tower, feat):
+        return remote(feat, feat_other.at[tower], core_send.at[tower, 0], core_recv.at[tower, 0], device(dc=1))
+
+    def proj_copy(tower):
+        cols = pl.ds(pl.multiple_of(lax.rem(core + 1, 2) * 512, 512), 512)
         return remote(
-            outer.at[tower, pl.ds(other * 4 + pair * 2, 2)], core_in.at[tower, pl.ds(pair * 2, 2)],
-            core_send.at[tower, order], core_recv.at[tower, order], device(dc=1),
+            proj_grad.at[tower, :, cols], proj_other.at[tower],
+            core_send.at[tower, 1], core_recv.at[tower, 1], device(dc=1),
         )
 
-    def weight_other(tower):
-        for order in range(2):
-            weight_part(tower, lax.rem(core + 1, 2), order)
-            launch(core_copy(tower, order))
-
-    def weight_own(tower):
-        for order in range(2):
-            weight_part(tower, core, order)
-
-    def one_copies(tower):
-        copies = []
-        for k in (2, 1, 3):
-            copies.append(remote(
-                half.at[tower, lax.rem(yy + k, 4), 0], y_in.at[tower, k - 1],
-                one_send.at[tower, 0], one_recv.at[tower, 0], device(dy=k),
-            ))
-            copies.append(remote(
-                half.at[tower, :, 1, lax.rem(xx + k, 4)], x_in.at[tower, k - 1],
-                one_send.at[tower, 1], one_recv.at[tower, 1], device(dx=k),
-            ))
-        return copies
+    def weight_part(tower, order):
+        pair = lax.rem(yy // 2 + 1 + order, 2)
+        own_cols = tile_at(core * 2 + pair, 256)
+        other_cols = tile_at(pair, 256)
+
+        def step(i, carry):
+            rows = tile_at(i, 512)
+            value = dot_nn(feat_t[tower, 0, rows, :], proj_grad[tower, :, own_cols])
+            value += dot_nn(feat_t[tower, 1, rows, :], proj_other[tower, :, other_cols])
+            value = value.astype(BF)
+            for z in range(4):
+                for q in range(2):
+                    for x in range(4):
+                        for route in range(2):
+                            first = z * 128 + x * 32 + route * 16
+                            half[tower, pair * 2 + q, route, x, i * 4 + z] = value[
+                                first : first + 16, q * 128 : q * 128 + 128
+                            ]
+            return carry
+
+        lax.fori_loop(0, 2, step, 0)
+
+    def y_copy(tower, k):
+        return remote(
+            half.at[tower, lax.rem(yy + k, 4), 0], y_in.at[tower, k - 1],
+            one_send.at[tower, 0], one_recv.at[tower, 0], device(dy=k),
+        )
+
+    def x_copy(tower, k):
+        return remote(
+            half.at[tower, :, 1, lax.rem(xx + k, 4)], x_in.at[tower, k - 1],
+            one_send.at[tower, 1], one_recv.at[tower, 1], device(dx=k),
+        )
+
+    def launch_some(tower, order):
+        if order == 0:
+            launch(y_copy(tower, 2))
+            launch(y_copy(tower, 3 - 2 * lax.rem(yy, 2)))
+        else:
+            for k in (2, 1, 3):
+                launch(x_copy(tower, k))
+            launch(y_copy(tower, 1 + 2 * lax.rem(yy, 2)))
 
     def two_copies(tower):
         copies = []
@@ -334,23 +336,6 @@
             copies.append(remote(view, view, send.at[tower, i], recv.at[tower, i], device(dc=1)))
         return copies
 
-    def stage_core_sum(tower, order):
-        pair = core_pair(order)
-        core_copy(tower, order).wait_recv()
-
-        def step(i, carry):
-            y = pair * 2 + i // 4
-            x = lax.rem(i, 4)
-            for route in range(2):
-                half[tower, y, route, x] = (
-                    outer[tower, core * 4 + y, route, x].astype(F32) + core_in[tower, y, route, x].astype(F32)
-                ).astype(BF)
-            return carry
-
-        lax.fori_loop(0, 8, step, 0)
-        if order == 1:
-            launch_all(one_copies(tower))
-
     def stage_one_sum(tower):
         for copy in stage_waits(tower, "one"):
             copy.wait_recv()
@@ -412,8 +397,10 @@
     project(0, feat_s, weight_s, store_score)
     pair = remote(score.at[0], score.at[1], side_send.at[0], side_recv.at[0], device(dx=2))
     launch(pair)
-    transpose(0, feat_s)
-    transpose(1, feat_a)
+    launch(feat_copy(0, feat_s))
+    launch(feat_copy(1, feat_a))
+    transpose(0, 0, feat_s)
+    transpose(1, 0, feat_a)
 
     for hop in range(1, 5):
         for chunk in CHUNKS:
@@ -426,6 +413,9 @@
         if hop == 1:
             pair.wait_recv()
             tile_grads(0, True)
+            for tower, feat in enumerate((feat_s, feat_a)):
+                feat_copy(tower, feat).wait_recv()
+                transpose(tower, 1, feat_other.at[tower])
         if hop < 4:
             tile_pair(hop)
         else:
@@ -441,42 +431,44 @@
     def store_own(cols, value):
         emb_grad[:, cols] = value
 
-    def near(hop):
+    side = remote(side_out, side_in, side_send.at[1], side_recv.at[1], device(dx=2))
+    def own_column(j):
+        return lambda: score_grad(0, store_own, j, 1)
+
+    def score_unit():
+        side.wait_recv()
+        unit_grad(0, lambda rows: emb_grad[rows, :] + side_in[rows, :].astype(F32), 0, ROWS)
+        launch(proj_copy(0))
+
+    def score_first():
+        proj_copy(0).wait_recv()
+        weight_part(0, 0)
+
+    def score_second():
+        weight_part(0, 1)
+        launch_some(0, 0)
+        launch_some(0, 1)
+
+    def score_back():
+        back(0, weight_s, back_s)
+
+    beside = {
+        0: own_column(0), 1: own_column(1), 2: own_column(2), 3: own_column(3),
+        6: score_unit, 7: score_first, 8: score_second, 9: score_back,
+        11: lambda: stage_one_sum(0),
+    }
+    takes = []
+    for hop, table in ((1, 1), (0, 0), (2, 1), (1, 0), (3, 1), (2, 0)):
         for k in range(2):
-            for way in (PLUS, MINUS):
-                ring_take(way, hop, SUM_FAR[1 - way][k])
-
-    def far(hop):
-        for k in range(2):
-            for way in (PLUS, MINUS):
-                ring_take(way, hop, SUM_FAR[way][k])
-
-    score_grad(1, store_side)
-    side = remote(side_out, side_in, side_send.at[1], side_recv.at[1], device(dx=2))
+            takes.append([(way, hop, SUM_FAR[way ^ table][k]) for way in (PLUS, MINUS)])
+
+    score_grad(1, store_side, 0, 4)
     launch(side)
-    near(1)
-    score_grad(0, store_own)
-    far(0)
-    near(2)
-    side.wait_recv()
-    unit_grad(0, lambda rows: emb_grad[rows, :] + side_in[rows, :].astype(F32), 0, ROWS)
-    weight_other(0)
-    far(1)
-    weight_own(0)
-    stage_core_sum(0, 0)
-    stage_core_sum(0, 1)
-    back(0, weight_s, back_s)
-    saves = [
-        pltpu.make_async_copy(src, dst, save_sem.at[i])
-        for i, (src, dst) in enumerate(
-            ((back_s, back_s_out), (back_a, back_a_out), (rows_s, rows_s_out), (rows_a, rows_a_out))
-        )
-    ]
-    saves[0].start()
-    near(3)
-    far(2)
-    stage_one_sum(0)
-    stage_two_sum(0)
+    for i, both in enumerate(takes):
+        for way, hop, chunk in both:
+            ring_take(way, hop, chunk)
+        if i in beside:
+            beside[i]()
 
     def audio_value(rows):
         return (
@@ -487,20 +479,20 @@
         for way in (PLUS, MINUS):
             ring_take(way, 3, SUM_FAR[way][k])
             unit_grad(1, audio_value, *SUM_FAR[way][k])
-    weight_other(1)
-    weight_own(1)
-    stage_core_sum(1, 0)
-    stage_core_sum(1, 1)
+    launch(proj_copy(1))
+    stage_two_sum(0)
+    proj_copy(1).wait_recv()
+    weight_part(1, 0)
+    launch_some(1, 0)
+    weight_part(1, 1)
+    launch_some(1, 1)
     back(1, weight_a, back_a)
-    saves[1].start()
+    stage_one_sum(1)
     stage_z_sum(0)
-    stage_one_sum(1)
+    stage_two_sum(1)
     stage_all(0, rows_s)
-    saves[2].start()
-    stage_two_sum(1)
     stage_z_sum(1)
     stage_all(1, rows_a)
-    saves[3].start()
 
     for way in (PLUS, MINUS):
         for hop in range(4):
@@ -514,25 +506,18 @@
     pair.wait_send()
     side.wait_send()
     for tower in range(2):
-        for order in range(2):
-            core_copy(tower, order).wait_send()
+        feat_copy(tower, (feat_s, feat_a)[tower]).wait_send()
+        proj_copy(tower).wait_send()
         for name in ("one", "two", "z", "all"):
             for copy in stage_waits(tower, name):
                 copy.wait_send()
-    for copy in saves:
-        copy.wait()
 
 
 def finish(*refs):
-    sources, targets, held, load, save = refs[:4], refs[4:8], refs[8:12], refs[12], refs[13]
-    loads = [pltpu.make_async_copy(sources[i], held[i], load.at[i]) for i in range(4)]
-    saves = [pltpu.make_async_copy(held[i], targets[i], save.at[i]) for i in range(4)]
-    for copy in loads:
+    copies = [pltpu.make_async_copy(refs[i], refs[4 + i], refs[8].at[i]) for i in range(4)]
+    for copy in copies:
         copy.start()
-    for i in range(4):
-        loads[i].wait()
-        saves[i].start()
-    for copy in saves:
+    for copy in copies:
         copy.wait()
 
 
@@ -550,13 +535,8 @@
         pltpu.SMEM((1,), F32),
         pltpu.SMEM((1,), F32),
         pltpu.SMEM((1,), F32),
-        pltpu.VMEM((ROWS, WIDTH), BF),
-        pltpu.VMEM((ROWS, WIDTH), BF),
-        pltpu.VMEM((64, WIDTH), F32),
-        pltpu.VMEM((64, WIDTH), F32),
-        pltpu.VMEM((2, WIDTH, ROWS), BF),
+        pltpu.VMEM((2, 2, WIDTH, ROWS), BF),
         dma((7,)),
-        dma((4,)),
         pltpu.VMEM((2, ROWS, WIDTH), F32),
         pltpu.VMEM((2, ROWS, 128), F32),
         pltpu.VMEM((8, ROWS, WIDTH), BF),
@@ -568,8 +548,8 @@
         pltpu.VMEM((ROWS, WIDTH), BF),
         pltpu.VMEM((ROWS, WIDTH), F32),
         pltpu.VMEM((2, ROWS, WIDTH), BF),
-        pltpu.VMEM((2, 8, 2, 4, 8, 16, 128), BF),
-        pltpu.VMEM((2, 4, 2, 4, 8, 16, 128), BF),
+        pltpu.VMEM((2, ROWS, WIDTH), BF),
+        pltpu.VMEM((2, ROWS, WIDTH // 2), BF),
         pltpu.VMEM((2, 4, 2, 4, 8, 16, 128), BF),
         pltpu.VMEM((2, 3, 4, 8, 16, 128), BF),
         pltpu.VMEM((2, 3, 4, 8, 16, 128), BF),
@@ -598,23 +578,27 @@
         dma((2, 1)),
     ]
     shapes = (rows, rows, sums, sums)
+    vmem = pl.BlockSpec(memory_space=pltpu.VMEM)
     results = pl.pallas_call(
         functools.partial(kernel, groups_rows),
-        out_shape=shapes,
+        out_shape=tuple(pltpu.VMEM(v.shape, v.dtype) for v in shapes),
         in_specs=[anywhere] * 7,
-        out_specs=(anywhere,) * 4,
+        out_specs=(vmem,) * 4,
         scratch_shapes=scratch,
         compiler_params=pltpu.CompilerParams(
-            collective_id=0, has_side_effects=True, vmem_limit_bytes=58 * 2**20
+            collective_id=0, has_side_effects=True, vmem_limit_bytes=52 * 2**20
         ),
-    )(score_feats[0], audio_feats[0], score_weight, audio_weight, log_temp, logit_bias, loss_scale)
+    )(*(
+        pltpu.with_memory_space_constraint(v, pltpu.HBM)
+        for v in (score_feats[0], audio_feats[0], score_weight, audio_weight)
+    ), log_temp, logit_bias, loss_scale)
     back_s, back_a, rows_s, rows_a = pl.pallas_call(
         finish,
         out_shape=shapes,
-        in_specs=[anywhere] * 4,
+        in_specs=[vmem] * 4,
         out_specs=(anywhere,) * 4,
-        scratch_shapes=[pltpu.VMEM(v.shape, v.dtype) for v in shapes] + [dma((4,)), dma((4,))],
-    )(*results)
+        scratch_shapes=[dma((4,))],
+    )(*(pltpu.with_memory_space_constraint(v, pltpu.VMEM) for v in results))
     return back_s[None], back_a[None], rows_s, rows_a
 
 

time: 122 us -> 116 us (0.951)
  Pallas kernels: 119 us -> 114 us
    pallas_call x2, Pallas kernels: 119 us -> 114 us  [the longest x1 112 us: body(): pl.pallas_call(functools.partial(kernel, groups_rows), out_shape=tuple((p...]
where the time goes in v3:
time: 116 us
  Pallas kernels  114 us (98%)
  between operations  2.58 us (2%)
    pallas_call x1, Pallas kernels, body(): pl.pallas_call(functools.partial(kernel, groups_rows), out_shape=tuple((p...  112 us

profile of v3, /device:TPU:1, one launch (start us, length us, event | category | flops | bytes accessed | tf_op | source)
XLA Modules:
  0.0 116.1 jit_solution(12941912416430934003)
XLA Ops:
  2.6 112.4 %shard_map.102 = (bf16[240,1024]{1,0:T(8,128)(2,1)S(1)}, bf16[240,1024]{1,0:T(8,128)(2,1)S(1)}, f32[64,1024]{1,0:T(8,128)S(1)}, f32[64,1024]{1,0:T(8,128)S(1)}) custom-call(bf16[240,1024]{1,0:T(8,128)(2,1)} %bitcast.4, bf16[240,1024]{1,0:T(8,128)(2,1)} %bitcast.5, bf16[1024,1024]{1,0:T(8,128)(2,1)} %weight_s_in.1, bf16[1024,1024]{1,0:T(8,128)(2,1)} %weight_a_in.1, ...), custom_call_target="tpu_custom_call" | custom-call | tf_op jit(solution)/shard_map/pallas_call | solution.py:582
  115.0 1.2 shard_map.103

commit v4 on v3

--- a/solution.py
+++ b/solution.py
@@ -41,9 +41,9 @@
 
 def kernel(
     groups_rows,
-    feat_s_in, feat_a_in, weight_s_in, weight_a_in, temp_in, bias_in, scale_in,
+    feat_s_in, feat_a_in, weight_s_in, weight_a_in, temp_ref, bias_ref, scale_ref,
     back_s, back_a, rows_s, rows_a,
-    feat_s, feat_a, weight_s, weight_a, temp_ref, bias_ref, scale_ref, feat_t,
+    feat_s, feat_a, weight_s, weight_a, feat_t,
     load_sem,
     unit, length, audio, score, grad_t, part, ring, side_out, side_in, emb_grad, proj_grad,
     feat_other, proj_other, half, y_in, x_in, y_sum, x_sum, x_in2, y_in2, z_out, z_in, done,
@@ -71,8 +71,8 @@
         )
 
     barrier = pltpu.get_barrier_semaphore()
-    peers = [device(dz=k) for k in range(1, 8)] + [flat_dp(k) for k in range(1, 16)]
-    peers += [device(dx=k) for k in (1, 2, 3)]
+    peers = [device(dz=1), device(dz=7), device(dc=1)]
+    peers += [device(dx=k) for k in (2, 1, 3)] + [device(dy=k) for k in (2, 1, 3)]
     for peer in peers:
         pl.semaphore_signal(barrier, inc=1, device_id=peer, device_id_type=MESH)
 
@@ -80,13 +80,10 @@
         pltpu.make_async_copy(src, dst, load_sem.at[i])
         for i, (src, dst) in enumerate((
             (feat_a_in, feat_a), (weight_a_in, weight_a), (feat_s_in, feat_s), (weight_s_in, weight_s),
-            (temp_in, temp_ref), (bias_in, bias_ref), (scale_in, scale_ref),
         ))
     ]
     for copy in loads:
         copy.start()
-    for copy in loads[4:]:
-        copy.wait()
 
     temper = jnp.exp(jnp.full((1, 1), temp_ref[0], F32))
     bias = bias_ref[0]
@@ -240,10 +237,10 @@
     def feat_copy(tower, feat):
         return remote(feat, feat_other.at[tower], core_send.at[tower, 0], core_recv.at[tower, 0], device(dc=1))
 
-    def proj_copy(tower):
+    def proj_copy(tower, first=0, count=ROWS):
         cols = pl.ds(pl.multiple_of(lax.rem(core + 1, 2) * 512, 512), 512)
         return remote(
-            proj_grad.at[tower, :, cols], proj_other.at[tower],
+            proj_grad.at[tower, pl.ds(first, count), cols], proj_other.at[tower, pl.ds(first, count)],
             core_send.at[tower, 1], core_recv.at[tower, 1], device(dc=1),
         )
 
@@ -275,33 +272,39 @@
             one_send.at[tower, 0], one_recv.at[tower, 0], device(dy=k),
         )
 
-    def x_copy(tower, k):
+    def x_copy(tower, order, k):
+        blocks = pl.ds(lax.rem(yy // 2 + 1 + order, 2) * 2, 2)
         return remote(
-            half.at[tower, :, 1, lax.rem(xx + k, 4)], x_in.at[tower, k - 1],
+            half.at[tower, blocks, 1, lax.rem(xx + k, 4)], x_in.at[tower, k - 1, blocks],
             one_send.at[tower, 1], one_recv.at[tower, 1], device(dx=k),
         )
 
     def launch_some(tower, order):
+        launch(x_copy(tower, order, 2))
         if order == 0:
             launch(y_copy(tower, 2))
             launch(y_copy(tower, 3 - 2 * lax.rem(yy, 2)))
         else:
-            for k in (2, 1, 3):
-                launch(x_copy(tower, k))
             launch(y_copy(tower, 1 + 2 * lax.rem(yy, 2)))
-
-    def two_copies(tower):
-        copies = []
-        for k in (2, 1, 3):
-            copies.append(remote(
-                y_sum.at[tower, lax.rem(xx + k, 4)], x_in2.at[tower, k - 1],
-                two_send.at[tower, 0], two_recv.at[tower, 0], device(dx=k),
-            ))
-            copies.append(remote(
+        launch(x_copy(tower, order, 1))
+        launch(x_copy(tower, order, 3))
+
+    def two_copies(tower, route):
+        if route == 0:
+            return [
+                remote(
+                    y_sum.at[tower, lax.rem(xx + k, 4)], x_in2.at[tower, k - 1],
+                    two_send.at[tower, 0], two_recv.at[tower, 0], device(dx=k),
+                )
+                for k in (2, 1, 3)
+            ]
+        return [
+            remote(
                 x_sum.at[tower, lax.rem(yy + k, 4)], y_in2.at[tower, k - 1],
                 two_send.at[tower, 1], two_recv.at[tower, 1], device(dy=k),
-            ))
-        return copies
+            )
+            for k in (2, 1, 3)
+        ]
 
     def z_copies(tower):
         return [
@@ -337,22 +340,29 @@
         return copies
 
     def stage_one_sum(tower):
-        for copy in stage_waits(tower, "one"):
-            copy.wait_recv()
-
-        def step(i, carry):
+        first, second = stage_waits(tower, "one")
+        first.wait_recv()
+
+        def y_step(i, carry):
             total = half[tower, yy, 0, i].astype(F32)
             for k in range(3):
                 total += y_in[tower, k, i].astype(F32)
             y_sum[tower, i] = total.astype(BF)
+            return carry
+
+        lax.fori_loop(0, 4, y_step, 0)
+        launch_all(two_copies(tower, 0))
+        second.wait_recv()
+
+        def x_step(i, carry):
             total = half[tower, i, 1, xx].astype(F32)
             for k in range(3):
                 total += x_in[tower, k, i].astype(F32)
             x_sum[tower, i] = total.astype(BF)
             return carry
 
-        lax.fori_loop(0, 4, step, 0)
-        launch_all(two_copies(tower))
+        lax.fori_loop(0, 4, x_step, 0)
+        launch_all(two_copies(tower, 1))
 
     def stage_two_sum(tower):
         for copy in stage_waits(tower, "two"):
@@ -479,7 +489,7 @@
         for way in (PLUS, MINUS):
             ring_take(way, 3, SUM_FAR[way][k])
             unit_grad(1, audio_value, *SUM_FAR[way][k])
-    launch(proj_copy(1))
+            launch(proj_copy(1, *SUM_FAR[way][k]))
     stage_two_sum(0)
     proj_copy(1).wait_recv()
     weight_part(1, 0)
@@ -524,6 +534,7 @@
 def body(score_feats, audio_feats, score_weight, audio_weight, log_temp, logit_bias, loss_scale):
     groups_rows = float(lax.axis_size("dp") * lax.axis_size("blk") * score_feats.shape[1])
     anywhere = pl.BlockSpec(memory_space=pl.ANY)
+    smem = pl.BlockSpec(memory_space=pltpu.SMEM)
     rows = jax.ShapeDtypeStruct((ROWS, WIDTH), BF)
     sums = jax.ShapeDtypeStruct((64, WIDTH), F32)
     dma = pltpu.SemaphoreType.DMA
@@ -532,11 +543,8 @@
         pltpu.VMEM((ROWS, WIDTH), BF),
         pltpu.VMEM((WIDTH, WIDTH), BF),
         pltpu.VMEM((WIDTH, WIDTH), BF),
-        pltpu.SMEM((1,), F32),
-        pltpu.SMEM((1,), F32),
-        pltpu.SMEM((1,), F32),
         pltpu.VMEM((2, 2, WIDTH, ROWS), BF),
-        dma((7,)),
+        dma((4,)),
         pltpu.VMEM((2, ROWS, WIDTH), F32),
         pltpu.VMEM((2, ROWS, 128), F32),
         pltpu.VMEM((8, ROWS, WIDTH), BF),
@@ -582,7 +590,7 @@
     results = pl.pallas_call(
         functools.partial(kernel, groups_rows),
         out_shape=tuple(pltpu.VMEM(v.shape, v.dtype) for v in shapes),
-        in_specs=[anywhere] * 7,
+        in_specs=[anywhere] * 4 + [smem] * 3,
         out_specs=(vmem,) * 4,
         scratch_shapes=scratch,
         compiler_params=pltpu.CompilerParams(

time: 116 us -> 115 us (level)
  no operation moved by 1% of the time
where the time goes in v4:
time: 115 us
  Pallas kernels  113 us (98%)
  between operations  2.58 us (2%)
    pallas_call x1, Pallas kernels, body(): pl.pallas_call(functools.partial(kernel, groups_rows), out_shape=tuple((p...  111 us

profile of v4, /device:TPU:1, one launch (start us, length us, event | category | flops | bytes accessed | tf_op | source)
XLA Modules:
  0.0 115.1 jit_solution(3173791428095122949)
XLA Ops:
  2.6 111.4 %shard_map.102 = (bf16[240,1024]{1,0:T(8,128)(2,1)S(1)}, bf16[240,1024]{1,0:T(8,128)(2,1)S(1)}, f32[64,1024]{1,0:T(8,128)S(1)}, f32[64,1024]{1,0:T(8,128)S(1)}) custom-call(bf16[240,1024]{1,0:T(8,128)(2,1)} %bitcast.4, bf16[240,1024]{1,0:T(8,128)(2,1)} %bitcast.5, bf16[1024,1024]{1,0:T(8,128)(2,1)} %weight_s_in.1, bf16[1024,1024]{1,0:T(8,128)(2,1)} %weight_a_in.1, ...), custom_call_target="tpu_custom_call" | custom-call | tf_op jit(solution)/shard_map/pallas_call | solution.py:590
  114.0 1.2 shard_map.103

commit v5 on v4

--- a/solution.py
+++ b/solution.py
@@ -468,9 +468,11 @@
         11: lambda: stage_one_sum(0),
     }
     takes = []
-    for hop, table in ((1, 1), (0, 0), (2, 1), (1, 0), (3, 1), (2, 0)):
-        for k in range(2):
-            takes.append([(way, hop, SUM_FAR[way ^ table][k]) for way in (PLUS, MINUS)])
+    for hop, table, k in (
+        (1, 1, 0), (1, 1, 1), (0, 0, 0), (0, 0, 1), (2, 1, 0), (1, 0, 0),
+        (1, 0, 1), (2, 1, 1), (3, 1, 0), (2, 0, 0), (2, 0, 1), (3, 1, 1),
+    ):
+        takes.append([(way, hop, SUM_FAR[way ^ table][k]) for way in (PLUS, MINUS)])
 
     score_grad(1, store_side, 0, 4)
     launch(side)
@@ -502,7 +504,6 @@
     stage_two_sum(1)
     stage_all(0, rows_s)
     stage_z_sum(1)
-    stage_all(1, rows_a)
 
     for way in (PLUS, MINUS):
         for hop in range(4):
@@ -518,9 +519,12 @@
     for tower in range(2):
         feat_copy(tower, (feat_s, feat_a)[tower]).wait_send()
         proj_copy(tower).wait_send()
-        for name in ("one", "two", "z", "all"):
+        for name in ("one", "two", "z", "all")[: 4 - tower]:
             for copy in stage_waits(tower, name):
                 copy.wait_send()
+    stage_all(1, rows_a)
+    for copy in stage_waits(1, "all"):
+        copy.wait_send()
 
 
 def finish(*refs):

time: 115 us -> 115 us (level)
  no operation moved by 1% of the time
where the time goes in v5:
time: 115 us
  Pallas kernels  112 us (97%)
  between operations  2.58 us (2%)
    pallas_call x1, Pallas kernels, body(): pl.pallas_call(functools.partial(kernel, groups_rows), out_shape=tuple((p...  111 us

profile of v5, /device:TPU:1, one launch (start us, length us, event | category | flops | bytes accessed | tf_op | source)
XLA Modules:
  0.0 114.9 jit_solution(16662983052562063937)
XLA Ops:
  2.6 111.2 %shard_map.102 = (bf16[240,1024]{1,0:T(8,128)(2,1)S(1)}, bf16[240,1024]{1,0:T(8,128)(2,1)S(1)}, f32[64,1024]{1,0:T(8,128)S(1)}, f32[64,1024]{1,0:T(8,128)S(1)}) custom-call(bf16[240,1024]{1,0:T(8,128)(2,1)} %bitcast.4, bf16[240,1024]{1,0:T(8,128)(2,1)} %bitcast.5, bf16[1024,1024]{1,0:T(8,128)(2,1)} %weight_s_in.1, bf16[1024,1024]{1,0:T(8,128)(2,1)} %weight_a_in.1, ...), custom_call_target="tpu_custom_call" | custom-call | tf_op jit(solution)/shard_map/pallas_call | solution.py:594
  113.8 1.2 %shard_map.103 = (bf16[240,1024]{1,0:T(8,128)(2,1)}, bf16[240,1024]{1,0:T(8,128)(2,1)}, f32[64,1024]{1,0:T(8,128)}, f32[64,1024]{1,0:T(8,128)}) custom-call(bf16[240,1024]{1,0:T(8,128)(2,1)S(1)} %get-tuple-element.12.refs_0_, bf16[240,1024]{1,0:T(8,128)(2,1)S(1)} %get-tuple-element.13.refs_1_, f32[64,1024]{1,0:T(8,128)S(1)} %get-tuple-element.14.refs_2_, ...), custom_call_target="tpu_custom_call" | custom-call | tf_op jit(solution)/shard_map/pallas_call | solution.py:607

commit v6 on v5

--- a/solution.py
+++ b/solution.py
@@ -20,6 +20,7 @@
 CHUNKS = LOW + HIGH
 PLUS, MINUS = 0, 1
 GATHER_FAR = {PLUS: HIGH, MINUS: LOW}
+GATHER_ORDER = {PLUS: HIGH + LOW, MINUS: LOW + HIGH}
 SUM_FAR = {PLUS: LOW, MINUS: HIGH}
 
 
@@ -399,9 +400,9 @@
     loads[1].wait()
     project(1, feat_a, weight_a, store_audio)
     pl.semaphore_wait(barrier, len(peers))
-    for chunk in CHUNKS:
+    for i in range(len(CHUNKS)):
         for way in (PLUS, MINUS):
-            launch(gather_copy(way, 1, chunk))
+            launch(gather_copy(way, 1, GATHER_ORDER[way][i]))
     loads[2].wait()
     loads[3].wait()
     project(0, feat_s, weight_s, store_score)
@@ -413,8 +414,9 @@
     transpose(1, 0, feat_a)
 
     for hop in range(1, 5):
-        for chunk in CHUNKS:
+        for i in range(len(CHUNKS)):
             for way in (PLUS, MINUS):
+                chunk = GATHER_ORDER[way][i]
                 if hop == 4 and chunk not in GATHER_FAR[way]:
                     continue
                 gather_copy(way, hop, chunk).wait_recv()

time: 115 us -> 115 us (level)
  no operation moved by 1% of the time
where the time goes in v6:
time: 115 us
  Pallas kernels  112 us (97%)
  between operations  2.58 us (2%)
    pallas_call x1, Pallas kernels, body(): pl.pallas_call(functools.partial(kernel, groups_rows), out_shape=tuple((p...  111 us

profile of v6, /device:TPU:1, one launch (start us, length us, event | category | flops | bytes accessed | tf_op | source)
XLA Modules:
  0.0 114.9 jit_solution(7116212207962826818)
XLA Ops:
  2.6 111.2 %shard_map.102 = (bf16[240,1024]{1,0:T(8,128)(2,1)S(1)}, bf16[240,1024]{1,0:T(8,128)(2,1)S(1)}, f32[64,1024]{1,0:T(8,128)S(1)}, f32[64,1024]{1,0:T(8,128)S(1)}) custom-call(bf16[240,1024]{1,0:T(8,128)(2,1)} %bitcast.4, bf16[240,1024]{1,0:T(8,128)(2,1)} %bitcast.5, bf16[1024,1024]{1,0:T(8,128)(2,1)} %weight_s_in.1, bf16[1024,1024]{1,0:T(8,128)(2,1)} %weight_a_in.1, ...), custom_call_target="tpu_custom_call" | custom-call | tf_op jit(solution)/shard_map/pallas_call | solution.py:596
  113.8 1.2 %shard_map.103 = (bf16[240,1024]{1,0:T(8,128)(2,1)}, bf16[240,1024]{1,0:T(8,128)(2,1)}, f32[64,1024]{1,0:T(8,128)}, f32[64,1024]{1,0:T(8,128)}) custom-call(bf16[240,1024]{1,0:T(8,128)(2,1)S(1)} %get-tuple-element.12.refs_0_, bf16[240,1024]{1,0:T(8,128)(2,1)S(1)} %get-tuple-element.13.refs_1_, f32[64,1024]{1,0:T(8,128)S(1)} %get-tuple-element.14.refs_2_, ...), custom_call_target="tpu_custom_call" | custom-call | tf_op jit(solution)/shard_map/pallas_call | solution.py:609
